TPU v7x, 256 devices: a whole 4x4x8 slice. The times are simulated.
256 devices in a mesh: group: 8 (over z), ctx: 32 (over x, y, core).
Axes of the slice: x: 4, y: 4, z: 8, core: 2. Of those that a mesh axis runs over, the one named last changes fastest.
Arguments:
- queries: bfloat16 [512, 8192], P(('group', 'ctx')), may hold values from -8 to 8
- prefix_keys: bfloat16 [16, 32768, 1024], P('group', 'ctx'), may hold values from -8 to 8
- prefix_values: bfloat16 [16, 32768, 1024], P('group', 'ctx'), may hold values from -6 to 6
- suffix_keys: bfloat16 [512, 256, 1024], P(('group', 'ctx')), may hold values from -8 to 8
- suffix_values: bfloat16 [512, 256, 1024], P(('group', 'ctx')), may hold values from -6 to 6
- new_keys: bfloat16 [512, 1024], P(('group', 'ctx')), may hold values from -8 to 8
- new_values: bfloat16 [512, 1024], P(('group', 'ctx')), may hold values from -6 to 6
- suffix_lengths: int32 [512], P(('group', 'ctx')), may hold values from 1 to 256
- counts: int32 [16], P('group'), may hold values from 1 to 63, as said below
- out_weight: bfloat16 [8192, 5120], P('ctx', 'group'), may hold values from -0.0625 to 0.0625
Outputs:
- projected: bfloat16 [512, 5120], P(('group', 'ctx'))
Inputs may be any that keep to these rules, and one draw needn't show every extreme that they name: `counts`: each group's 2 consecutive entries sum to 64; the samples of a group stand in the order of its prompts.
All inputs are finite; a program needn't handle non-finite values.
Results may differ from a plain program's by a relative error of at most 0.0058.
Values may be sent and summed in bfloat16 or wider, within the bound.
No kernel may reach another device: no remote copies, remote signals or barrier semaphores. Data moves between devices by JAX's collectives and lax.ppermute only.
A program may use at most 128 MiB of HBM per device.

v0:
```python
import math

import jax
import jax.numpy as jnp
import numpy as np
from jax import lax
from jax.experimental import pallas as pl
from jax.experimental.pallas import tpu as pltpu
from jax.sharding import PartitionSpec as P

QH = 64
KVH = 8
DH = 128
GQ = QH // KVH
CHIP_HEADS = 4
MASS_ROWS = 16
FLOOR = -1e30
SCALE = 1.0 / math.sqrt(DH)
ROWS = 16
TILE = ROWS * GQ
SPLITS = (5, 3)
CONTRACT = (((1,), (1,)), ((), ()))


def suffix_kernel(len_ref, info_ref, q_hbm, sk_hbm, sv_hbm, nk_hbm, nv_hbm, out_ref, q_ref, sk_ref, sv_ref, nk_ref, nv_ref, sems):
    pairs = (
        (q_hbm, q_ref),
        (nk_hbm, nk_ref),
        (nv_hbm, nv_ref),
        (sk_hbm, sk_ref),
        (sv_hbm, sv_ref),
    )
    copies = [pltpu.make_async_copy(a, b, sems.at[i]) for i, (a, b) in enumerate(pairs)]
    for c in copies:
        c.start()
    for c in copies:
        c.wait()
    samp, suf, _ = sk_ref.shape
    rows = GQ * samp
    row_samp = lax.broadcasted_iota(jnp.int32, (rows, suf), 0) % samp
    pos = lax.broadcasted_iota(jnp.int32, (rows, suf), 1)
    own = lax.broadcasted_iota(jnp.int32, (rows, DH), 0) % samp
    for h in range(KVH):
        cols = slice(h * DH, (h + 1) * DH)
        q = jnp.concatenate(
            [
                q_ref[:, (h * GQ + g) * DH : (h * GQ + g + 1) * DH].astype(jnp.float32)
                for g in range(GQ)
            ],
            axis=0,
        )
        q16 = q.astype(jnp.bfloat16)
        scores = []
        for j in range(samp):
            s = lax.dot_general(
                q16, sk_ref[j, :, cols], CONTRACT, preferred_element_type=jnp.float32
            )
            seen = (row_samp == j) & (pos < len_ref[j])
            scores.append(jnp.where(seen, s * SCALE, FLOOR))
        nk = jnp.zeros((rows, DH), jnp.float32)
        nv = jnp.zeros((rows, DH), jnp.float32)
        for j in range(samp):
            nk = jnp.where(own == j, nk_ref[j : j + 1, cols].astype(jnp.float32), nk)
            nv = jnp.where(own == j, nv_ref[j : j + 1, cols].astype(jnp.float32), nv)
        self_score = jnp.sum(q * nk, axis=1, keepdims=True) * SCALE
        peak = self_score
        for s in scores:
            peak = jnp.maximum(peak, jnp.max(s, axis=1, keepdims=True))
        self_term = jnp.exp(self_score - peak)
        total = self_term
        acc = self_term.astype(jnp.bfloat16).astype(jnp.float32) * nv
        for j in range(samp):
            terms = jnp.exp(scores[j] - peak)
            total = total + jnp.sum(terms, axis=1, keepdims=True)
            acc = acc + jnp.dot(
                terms.astype(jnp.bfloat16), sv_ref[j, :, cols], preferred_element_type=jnp.float32
            )
        out_ref[h, :, 0:DH] = acc
        out_ref[h, :, DH : 2 * DH] = jnp.broadcast_to(peak, (rows, DH))
        out_ref[h, :, 2 * DH : 3 * DH] = jnp.broadcast_to(total, (rows, DH))


def spread_kernel(q_ref, out_ref):
    for d in range(out_ref.shape[0]):
        out_ref[d] = q_ref[...]


def mass_block(mass, rows):
    high = mass.astype(jnp.bfloat16).astype(jnp.float32)
    mid = (mass - high).astype(jnp.bfloat16).astype(jnp.float32)
    row = lax.broadcasted_iota(jnp.int32, (rows, DH), 0)
    block = jnp.where(row == 0, high, jnp.where(row == 1, mid, mass - high - mid))
    return jnp.where(row < 3, block, 0.0)


def read_mass(ref):
    block = ref[:, ref.shape[1] - MASS_ROWS :, :].astype(jnp.float32)
    return block[:, 0] + block[:, 1] + block[:, 2]


def as_columns(x):
    parts = x.shape[0]
    return jnp.concatenate([x, jnp.zeros((DH - parts, DH), jnp.float32)], axis=0).T


def prefix_kernel(
    info_ref,
    counts_ref,
    q_own,
    q_oth,
    k_ref,
    v_ref,
    suf_ref,
    keep_ref,
    send_ref,
    acc_ref,
    peak_ref,
    total_ref,
):
    core = info_ref[0]
    positions = k_ref.shape[1]
    rows = q_own.shape[0]
    tiles = rows // ROWS
    visits = []
    for side, q_ref in enumerate((q_own, q_oth)):
        left = jnp.maximum(counts_ref[0] - 2 * (core if side == 0 else 1 - core), 0)
        count = 2 * (left // 4) + jnp.minimum(left % 4, 2)
        both = jnp.minimum(count // ROWS, tiles - 1)
        for i in range(tiles - 1):
            prompt = (i >= both).astype(jnp.int32)
            visits.append((side, q_ref, i + prompt, [prompt], count))
        visits.append((side, q_ref, both, [0, 1], count))

    def scores(visit):
        _, q_ref, tile, prompts, count = visit
        base = pl.multiple_of(tile * ROWS, ROWS)
        q = jnp.concatenate(
            [q_ref[pl.ds(base, ROWS), g * DH : (g + 1) * DH] for g in range(GQ)], axis=0
        )
        s = [
            lax.dot_general(q, k_ref[p], CONTRACT, preferred_element_type=jnp.float32)
            for p in prompts
        ]
        if len(s) == 1:
            return s[0]
        row = lax.broadcasted_iota(jnp.int32, (TILE, positions), 0) % ROWS + base
        return jnp.where(row < count, s[0], s[1])

    def weights(s, peak):
        terms = jnp.exp((s - peak) * SCALE)
        return terms.astype(jnp.bfloat16), peak, jnp.sum(terms, axis=1, keepdims=True)

    def values(visit, terms, peak, total):
        side, _, tile, prompts, count = visit
        acc = [jnp.dot(terms, v_ref[p], preferred_element_type=jnp.float32) for p in prompts]
        if len(acc) == 2:
            row = lax.broadcasted_iota(jnp.int32, (TILE, DH), 0) % ROWS + tile * ROWS
            acc = [jnp.where(row < count, acc[0], acc[1])]
        at = side * tiles + tile
        acc_ref[at] = acc[0]
        peak_ref[at] = jnp.broadcast_to(peak * SCALE, (TILE, DH))
        total_ref[at] = jnp.broadcast_to(total, (TILE, DH))

    def scored(visit):
        s = scores(visit)
        return s, jnp.max(s, axis=1, keepdims=True)

    ahead = scored(visits[0])
    behind = None
    for i, visit in enumerate(visits):
        now = ahead
        if i + 1 < len(visits):
            ahead = scored(visits[i + 1])
        if behind is not None:
            values(*behind)
        behind = (visit,) + weights(*now)
    values(*behind)

    home_tile = info_ref[1]
    home_row = info_ref[2]
    row = lax.broadcasted_iota(jnp.int32, (ROWS, DH), 0)
    for g in range(GQ):
        part = slice(g * ROWS, (g + 1) * ROWS)
        add = jnp.zeros((ROWS, DH), jnp.float32)
        add_peak = jnp.full((ROWS, DH), FLOOR, jnp.float32)
        add_total = jnp.zeros((ROWS, DH), jnp.float32)
        for j in range(2):
            here = row == home_row + j
            line = slice(2 * g + j, 2 * g + j + 1)
            add = jnp.where(here, suf_ref[0, line, 0:DH], add)
            add_peak = jnp.where(here, suf_ref[0, line, DH : 2 * DH], add_peak)
            add_total = jnp.where(here, suf_ref[0, line, 2 * DH : 3 * DH], add_total)
        peak = peak_ref[home_tile, part, :]
        top = jnp.maximum(peak, add_peak)
        a = jnp.exp(peak - top)
        b = jnp.exp(add_peak - top)
        acc_ref[home_tile, part, :] = acc_ref[home_tile, part, :] * a + add * b
        total_ref[home_tile, part, :] = total_ref[home_tile, part, :] * a + add_total * b
        peak_ref[home_tile, part, :] = top

    lane = lax.broadcasted_iota(jnp.int32, (ROWS, DH), 1)
    lines = [[None] * (CHIP_HEADS * tiles) for _ in range(4)]
    for side, out_ref in enumerate((keep_ref, send_ref)):
        for t in range(tiles):
            for g in range(GQ):
                chip, h = g // CHIP_HEADS, g % CHIP_HEADS
                part = slice(g * ROWS, (g + 1) * ROWS)
                total = total_ref[side * tiles + t, part, :]
                avg = acc_ref[side * tiles + t, part, :] / total
                at = h * rows + t * ROWS
                out_ref[chip, at : at + ROWS, :] = avg.astype(out_ref.dtype)
                lines[2 * side + chip][h * tiles + t] = peak_ref[
                    side * tiles + t, part, :
                ] + jnp.log(total)
    table = []
    for i in range(CHIP_HEADS * tiles):
        block = lines[0][i]
        for c in range(1, 4):
            block = jnp.where(lane == c, lines[c][i], block)
        table.append(block)
    table = jnp.concatenate(table, axis=0).T
    for side, out_ref in enumerate((keep_ref, send_ref)):
        for chip in range(2):
            c = 2 * side + chip
            block = mass_block(table[c : c + 1], MASS_ROWS)
            out_ref[chip, CHIP_HEADS * rows :, :] = block.astype(out_ref.dtype)


def join_kernel(*refs):
    out_ref = refs[-1]
    calls = len(SPLITS)
    at = 0
    for keep_ref, recv_ref in zip(refs[:calls], refs[calls : 2 * calls]):
        parts = keep_ref.shape[0]
        lines = keep_ref.shape[1] - MASS_ROWS
        masses = [read_mass(ref) for ref in (keep_ref, recv_ref)]
        top = jnp.maximum(*masses)
        shares = [jnp.exp(m - top) for m in masses]
        total = shares[0] + shares[1]
        weights = [as_columns(x / total) for x in shares]
        mass = top + jnp.log(total)
        for p in range(parts):
            a, b = [w[:, p : p + 1] for w in weights]
            acc = a * keep_ref[p, :lines, :] + b * recv_ref[p, :lines, :].astype(jnp.float32)
            out_ref[at + p, :lines, :] = acc.astype(jnp.bfloat16)
            block = mass_block(mass[p : p + 1], MASS_ROWS)
            out_ref[at + p, lines:, :] = block.astype(jnp.bfloat16)
        at += parts


def project_kernel(info_ref, parts_ref, *rest):
    blocks, out_ref = rest[:-1], rest[-1]
    core = info_ref[0]
    parts = parts_ref.shape[0]
    lines = parts_ref.shape[1] - MASS_ROWS
    rows = lines // CHIP_HEADS
    mass = read_mass(parts_ref)
    share = jnp.exp(mass - jnp.max(mass, axis=0, keepdims=True))
    flat = as_columns(share / jnp.sum(share, axis=0, keepdims=True))
    acc = jnp.zeros((lines, DH), jnp.float32)
    for p in range(parts):
        acc = acc + flat[:, p : p + 1] * parts_ref[p, :lines, :].astype(jnp.float32)
    heads = [acc[h * rows : (h + 1) * rows] for h in range(CHIP_HEADS)]
    half = CHIP_HEADS // 2
    first = jnp.concatenate(heads[:half], axis=1)
    second = jnp.concatenate(heads[half:], axis=1)
    own = jnp.where(core == 0, first, second).astype(jnp.bfloat16)
    oth = jnp.where(core == 0, second, first).astype(jnp.bfloat16)
    own_first = jnp.concatenate([own, oth], axis=1)
    oth_first = jnp.concatenate([oth, own], axis=1)
    cols = blocks[0].shape[1]
    plan = [((own, blocks[0]), (oth, blocks[1]))]
    plan += [((oth_first if i in (1, 3, 5) else own_first, b),) for i, b in enumerate(blocks[2:])]
    for i, terms in enumerate(plan):
        out = sum(jnp.dot(a, w[...], preferred_element_type=jnp.float32) for a, w in terms)
        to = pl.multiple_of(info_ref[3 + i] * cols, DH)
        for chip in range(out_ref.shape[0]):
            out_ref[chip, :, pl.ds(to, cols)] = out[2 * chip : 2 * chip + 2].astype(jnp.bfloat16)


def body(
    queries,
    prefix_keys,
    prefix_values,
    suffix_keys,
    suffix_values,
    new_keys,
    new_values,
    suffix_lengths,
    counts,
    out_weight,
):
    bf16, f32, i32 = jnp.bfloat16, jnp.float32, jnp.int32
    samp = queries.shape[0]
    n_ctx = lax.axis_size("ctx")
    n_grp = lax.axis_size("group")
    chips = n_ctx // 2
    me = lax.axis_index("ctx")
    z = lax.axis_index("group")
    rows = samp * chips
    same_core = [[2 * d + k for d in range(chips)] for k in range(2)]

    def other_core(x):
        return lax.ppermute(x, "ctx", [(i, i ^ 1) for i in range(n_ctx)])

    def along_z(x):
        ring = [
            (g * n_ctx + c, (g + (1 if c % 2 == 0 else -1)) % n_grp * n_ctx + c)
            for g in range(n_grp)
            for c in range(n_ctx)
        ]
        return lax.ppermute(x, ("group", "ctx"), ring)

    def after(x, *earlier):
        return lax.optimization_barrier((x,) + earlier)[0]

    vmem = pl.BlockSpec(memory_space=pltpu.VMEM)
    smem = pl.BlockSpec(memory_space=pltpu.SMEM)
    hbm = pl.BlockSpec(memory_space=pl.ANY)

    with jax.named_scope("spread_queries"):
        spread = pl.pallas_call(
            spread_kernel,
            out_shape=jax.ShapeDtypeStruct((chips,) + queries.shape, bf16),
            in_specs=[vmem],
            out_specs=vmem,
            cost_estimate=pl.CostEstimate(flops=1, bytes_accessed=2**19, transcendentals=0),
        )(queries)
        q_own = lax.all_to_all(spread, "ctx", 0, 0, tiled=True, axis_index_groups=same_core)
        q_own = q_own.reshape(rows, QH * DH)

    with jax.named_scope("weights"):
        w_oth = other_core(out_weight)
        x1_own = along_z(out_weight)
        x1_oth = along_z(w_oth)

    table = []
    for g in range(n_grp):
        for c in range(n_ctx):
            way = 1 - 2 * (c % 2)
            home = samp * (c // 2)
            origin = [(g - way * by) % n_grp for by in (0, 1, -1, 2, -2, 3, -3, 4)]
            table.append([c % 2, home // ROWS, home % ROWS] + origin)
    info = lax.dynamic_index_in_dim(
        jnp.asarray(np.array(table, np.int32)), z * n_ctx + me, 0, keepdims=False
    )

    with jax.named_scope("suffix"):
        given = (queries, suffix_keys, suffix_values, new_keys, new_values)
        suffix = pl.pallas_call(
            suffix_kernel,
            out_shape=jax.ShapeDtypeStruct((KVH, GQ * samp, 3 * DH), f32),
            in_specs=[smem, smem] + [hbm] * 5,
            out_specs=vmem,
            scratch_shapes=[pltpu.VMEM(x.shape, x.dtype) for x in given]
            + [pltpu.SemaphoreType.DMA((5,))],
            compiler_params=pltpu.CompilerParams(vmem_limit_bytes=56 * 2**20),
            cost_estimate=pl.CostEstimate(flops=1, bytes_accessed=1, transcendentals=1),
        )(suffix_lengths, info, *given)

    with jax.named_scope("weights"):
        x1 = jnp.concatenate([x1_own, x1_oth], axis=0)

    with jax.named_scope("spread_queries"):
        q_oth = other_core(after(q_own, suffix, x1))

    with jax.named_scope("weights"):
        x2 = along_z(x1)
        e1 = other_core(x1)

    keeps, recvs = [], []
    with jax.named_scope("prefix"):
        prompts, positions, _ = prefix_keys.shape
        sent_rows = CHIP_HEADS * rows + MASS_ROWS
        tiles = 2 * rows // ROWS
        for n, heads in enumerate(SPLITS):
            at = sum(SPLITS[:n])
            q_block = pl.BlockSpec((rows, GQ * DH), lambda j, at=at: (0, at + j))
            kv_block = pl.BlockSpec(
                (prompts, positions, DH), lambda j, at=at: (0, 0, at + j)
            )
            suf_block = pl.BlockSpec(
                (1, GQ * samp, 3 * DH), lambda j, at=at: (at + j, 0, 0)
            )
            out_block = pl.BlockSpec((2, sent_rows, DH), lambda j: (j, 0, 0))
            keep, send = pl.pallas_call(
                prefix_kernel,
                out_shape=(
                    jax.ShapeDtypeStruct((2 * heads, sent_rows, DH), f32),
                    jax.ShapeDtypeStruct((2 * heads, sent_rows, DH), bf16),
                ),
                grid=(heads,),
                in_specs=[smem, smem, q_block, q_block, kv_block, kv_block, suf_block],
                out_specs=(out_block, out_block),
                scratch_shapes=[pltpu.VMEM((tiles, TILE, DH), f32)] * 3,
                compiler_params=pltpu.CompilerParams(vmem_limit_bytes=52 * 2**20),
                cost_estimate=pl.CostEstimate(
                    flops=2**31, bytes_accessed=2**23, transcendentals=2**22
                ),
            )(info, counts, q_own, q_oth, prefix_keys, prefix_values, suffix)
            keeps.append(keep)
            if n == 0:
                q_own, q_oth, x2, e1, send = lax.optimization_barrier(
                    (q_own, q_oth, x2, e1, send)
                )
            recvs.append(other_core(send))

    with jax.named_scope("weights"):
        x3 = along_z(x2)
        e2 = other_core(x2)

    with jax.named_scope("join_cores"):
        parts = pl.pallas_call(
            join_kernel,
            out_shape=jax.ShapeDtypeStruct((chips, sent_rows, DH), bf16),
            in_specs=[vmem] * (2 * len(SPLITS)),
            out_specs=vmem,
            compiler_params=pltpu.CompilerParams(vmem_limit_bytes=24 * 2**20),
        )(*keeps, *recvs)

    with jax.named_scope("weights"):
        parts, x3, e2 = lax.optimization_barrier((parts, x3, e2))
        e3 = other_core(x3)
        x4 = along_z(x3)
        blocks = (out_weight, w_oth, x1, e1, x2, e2, x3, e3, x4)

    with jax.named_scope("send_parts"):
        parts = lax.all_to_all(parts, "ctx", 0, 0, tiled=True, axis_index_groups=same_core)

    with jax.named_scope("project"):
        width = out_weight.shape[1]
        out = pl.pallas_call(
            project_kernel,
            out_shape=jax.ShapeDtypeStruct((chips, samp, n_grp * width), bf16),
            in_specs=[smem] + [vmem] * (1 + len(blocks)),
            out_specs=vmem,
            compiler_params=pltpu.CompilerParams(vmem_limit_bytes=20 * 2**20),
            cost_estimate=pl.CostEstimate(
                flops=2**28, bytes_accessed=2**23, transcendentals=2**12
            ),
        )(info, parts, *blocks)

    with jax.named_scope("send_rows"):
        out = lax.all_to_all(out, "ctx", 0, 0, tiled=True, axis_index_groups=same_core)
        return jnp.sum(out.astype(f32), axis=0).astype(bf16)


def solution(mesh):
    in_specs = (
        P(("group", "ctx"), None),
        P("group", "ctx", None),
        P("group", "ctx", None),
        P(("group", "ctx"), None, None),
        P(("group", "ctx"), None, None),
        P(("group", "ctx"), None),
        P(("group", "ctx"), None),
        P(("group", "ctx")),
        P("group"),
        P("ctx", "group"),
    )
    out_specs = P(("group", "ctx"), None)
    return jax.shard_map(body, mesh=mesh, in_specs=in_specs, out_specs=out_specs, check_vma=False)
```

profile of v0, /device:TPU:96, one launch (start us, length us, event | category | flops | bytes accessed | tf_op | source)
XLA Modules:
  0.0 82.8 jit_solution(7697092220794541466)
XLA Ops:
  0.0 1.6 %spread_queries.1 = bf16[16,2,8192]{2,1,0:T(2,128)(2,1)} custom-call(bf16[2,8192]{1,0:T(2,128)(2,1)} %q_hbm.1), custom_call_target="tpu_custom_call" | custom-call | flops 1 | bytes 524288 | tf_op jit(solution)/shard_map/spread_queries/pallas_call | solution.py:322
  1.6 7.0 %all-to-all-start = ((bf16[16,2,8192]{2,1,0:T(2,128)(2,1)}), bf16[16,2,8192]{2,1,0:T(2,128)(2,1)S(1)}, u32[]{:S(2)}, u32[]{:S(2)}) async-start(bf16[16,2,8192]{2,1,0:T(2,128)(2,1)} %spread_queries.1), calls=%async_computation | async-start | bytes 1048576 | tf_op jit(solution)/shard_map/spread_queries/all_to_all | solution.py:329
  8.7 3.2 %collective-permute-start = (bf16[256,640]{1,0:T(8,128)(2,1)}, bf16[256,640]{1,0:T(8,128)(2,1)S(1)}, u32[]{:S(2)}, u32[]{:S(2)}) collective-permute-start(bf16[256,640]{1,0:T(8,128)(2,1)} %rest_0_.1), channel_id=1, source_target_pairs={{0,32},{1,225},{2,34},{3,227},{4,36},{5,229},{6,38},{7,231},{8,40}... | collective-permute-start | bytes 983048 | tf_op jit(solution)/shard_map/weights/ppermute | solution.py:312
  11.9 1.0 %collective-permute-start.2 = (bf16[256,640]{1,0:T(8,128)(2,1)S(1)}, bf16[256,640]{1,0:T(8,128)(2,1)S(1)}, u32[]{:S(2)}, u32[]{:S(2)}) collective-permute-start(bf16[256,640]{1,0:T(8,128)(2,1)S(1)} %collective-permute-done.1.rest_1_), channel_id=1, source_target_pairs={{0,32},{1,225},{2,34},{3,227},{4,36},{5,229},{6,38},{7,231},{8,40}... | collective-permute-start | bytes 983048 | tf_op jit(solution)/shard_map/weights/ppermute | solution.py:312
  12.9 1.2 %dynamic-slice_bitcast_fusion.info_ref = s32[11]{0:T(128)} fusion(s32[256,11]{1,0:T(8,128)} %constant.22.clone, s32[]{:T(128)S(6)} %select_n.4), kind=kLoop, calls=%fused_computation.2 | loop fusion | bytes 92 | tf_op jit(solution)/shard_map/jit(dynamic_index_in_dim)/squeeze | solution.py:344
  14.1 5.2 %suffix.1.suf_ref = f32[8,16,384]{2,1,0:T(8,128)} custom-call(s32[2]{0:T(128)} %len_ref.1, s32[11]{0:T(128)} %dynamic-slice_bitcast_fusion.info_ref, bf16[2,8192]{1,0:T(2,128)(2,1)} %q_hbm.1, bf16[2,256,1024]{2,1,0:T(8,128)(2,1)} %sk_hbm.1, bf16[2,256,1024]{2,1,0:T(8,128)(2,1)} %sv_hbm.1, bf16[2,1024]{1,0:T(2,128)(2,1)} %nk_hbm.1, bf16[2,1024]{1,0:T(2,128)(2,1)} %nv_hbm.1), custom_call_target="tpu_custom_call" | custom-call | flops 1 | bytes 1 | tf_op jit(solution)/shard_map/suffix/pallas_call | solution.py:350
  19.3 1.5 %all-to-all-done = bf16[16,2,8192]{2,1,0:T(2,128)(2,1)S(1)} async-done(((bf16[16,2,8192]{2,1,0:T(2,128)(2,1)}), bf16[16,2,8192]{2,1,0:T(2,128)(2,1)S(1)}, u32[]{:S(2)}, u32[]{:S(2)}) %all-to-all-start) | async-done | bytes 524320 | tf_op jit(solution)/shard_map/spread_queries/all_to_all | solution.py:329
  20.8 0.2 reshape.3.q_own
  21.1 0.1 collective-permute-start.3
  21.2 0.5 collective-permute-start.5
  21.7 3.1 %collective-permute-start.4 = (bf16[512,640]{1,0:T(8,128)(2,1)S(1)}, bf16[512,640]{1,0:T(8,128)(2,1)S(1)}, u32[]{:S(2)}, u32[]{:S(2)}) collective-permute-start(bf16[512,640]{1,0:T(8,128)(2,1)S(1)} %constant_dynamic-update-slice_fusion.rest_2_), channel_id=1, source_target_pairs={{0,32},{1,225},{2,34},{3,227},{4,36},{5,229},{6,38},{7,231},{8,40}... | collective-permute-start | bytes 1966088 | tf_op jit(solution)/shard_map/weights/ppermute | solution.py:312
  24.8 0.9 %copy-done = f32[8,16,384]{2,1,0:T(8,128)S(1)} copy-done((f32[8,16,384]{2,1,0:T(8,128)S(1)}, f32[8,16,384]{2,1,0:T(8,128)}, u32[]{:S(2)}) %copy-start) | copy-done | bytes 196632
  25.7 8.8 %prefix.2 = (f32[10,144,128]{2,1,0:T(8,128)}, bf16[10,144,128]{2,1,0:T(8,128)(2,1)S(1)}) custom-call(s32[11]{0:T(128)S(1)} %copy-done.3, s32[2]{0:T(128)S(1)} %copy-done.4, bf16[32,8192]{1,0:T(8,128)(2,1)S(1)} %reshape.3.q_own, bf16[32,8192]{1,0:T(8,128)(2,1)S(1)} %collective-permute-done.3.q_oth, bf16[2,1024,1024]{2,1,0:T(8,128)(2,1)} %k_ref.3, ...), custom_call_target="tpu_custom_call" | custom-call | flops 2147483648 | bytes 8388608 | tf_op jit(solution)/shard_map/prefix/pallas_call | solution.py:386
  34.6 2.0 %collective-permute-start.8 = (bf16[512,640]{1,0:T(8,128)(2,1)S(1)}, bf16[512,640]{1,0:T(8,128)(2,1)S(1)}, u32[]{:S(2)}, u32[]{:S(2)}) collective-permute-start(bf16[512,640]{1,0:T(8,128)(2,1)S(1)} %collective-permute-done.4.rest_4_), channel_id=1, source_target_pairs={{0,32},{1,225},{2,34},{3,227},{4,36},{5,229},{6,38},{7,231},{8,40}... | collective-permute-start | bytes 1966088 | tf_op jit(solution)/shard_map/weights/ppermute | solution.py:312
  36.7 5.3 %prefix.3 = (f32[6,144,128]{2,1,0:T(8,128)S(1)}, bf16[6,144,128]{2,1,0:T(8,128)(2,1)S(1)}) custom-call(s32[11]{0:T(128)S(1)} %copy-done.3, s32[2]{0:T(128)S(1)} %copy-done.4, bf16[32,8192]{1,0:T(8,128)(2,1)S(1)} %reshape.3.q_own, bf16[32,8192]{1,0:T(8,128)(2,1)S(1)} %collective-permute-done.3.q_oth, bf16[2,1024,1024]{2,1,0:T(8,128)(2,1)} %k_ref.3, ...), custom_call_target="tpu_custom_call" | custom-call | flops 2147483648 | bytes 8388608 | tf_op jit(solution)/shard_map/prefix/pallas_call | solution.py:386
  42.0 0.6 collective-permute-start.7
  42.6 1.1 %collective-permute-done.7.refs_3_ = bf16[6,144,128]{2,1,0:T(8,128)(2,1)S(1)} collective-permute-done((bf16[6,144,128]{2,1,0:T(8,128)(2,1)S(1)}, bf16[6,144,128]{2,1,0:T(8,128)(2,1)S(1)}, u32[]{:S(2)}, u32[]{:S(2)}) %collective-permute-start.7) | collective-permute-done | bytes 221216 | tf_op jit(solution)/shard_map/prefix/ppermute | solution.py:304
  43.7 0.9 %join_cores.1 = bf16[16,144,128]{2,1,0:T(8,128)(2,1)S(1)} custom-call(f32[10,144,128]{2,1,0:T(8,128)S(1)} %copy-done.1, f32[6,144,128]{2,1,0:T(8,128)S(1)} %get-tuple-element.23.refs_1_, bf16[10,144,128]{2,1,0:T(8,128)(2,1)S(1)} %collective-permute-done.6.refs_2_, bf16[6,144,128]{2,1,0:T(8,128)(2,1)S(1)} %collective-permute-done.7.refs_3_), custom_call_target="tpu_custom_call" | custom-call | tf_op jit(solution)/shard_map/join_cores/pallas_call | solution.py:413
  44.6 0.7 collective-permute-done.8.rest_6_
  45.3 3.2 %collective-permute-start.11 = (bf16[512,640]{1,0:T(8,128)(2,1)S(1)}, bf16[512,640]{1,0:T(8,128)(2,1)S(1)}, u32[]{:S(2)}, u32[]{:S(2)}) collective-permute-start(bf16[512,640]{1,0:T(8,128)(2,1)S(1)} %collective-permute-done.8.rest_6_), channel_id=1, source_target_pairs={{0,32},{1,225},{2,34},{3,227},{4,36},{5,229},{6,38},{7,231},{8,40}... | collective-permute-start | bytes 1966088 | tf_op jit(solution)/shard_map/weights/ppermute | solution.py:312
  48.5 19.5 %all_to_all.15.parts_ref = bf16[16,144,128]{2,1,0:T(8,128)(2,1)S(1)} all-to-all(bf16[16,144,128]{2,1,0:T(8,128)(2,1)S(1)} %join_cores.1), channel_id=1, replica_groups={{0,2,4,6,8,10,12,14,16,18,20,22,24,26,28,30},{1,3,5,7,9,11,13,15,17,19,..., dimensions={0} | all-to-all | bytes 1179648 | tf_op jit(solution)/shard_map/send_parts/all_to_all | solution.py:428
  68.0 1.9 %project.1 = bf16[16,2,5120]{2,1,0:T(2,128)(2,1)S(1)} custom-call(s32[11]{0:T(128)S(1)} %copy-done.3, bf16[16,144,128]{2,1,0:T(8,128)(2,1)S(1)} %all_to_all.15.parts_ref, bf16[256,640]{1,0:T(8,128)(2,1)S(1)} %copy-done.2, bf16[256,640]{1,0:T(8,128)(2,1)S(1)} %collective-permute-done.1.rest_1_, ...), custom_call_target="tpu_custom_call" | custom-call | flops 268435456 | bytes 8388608 | tf_op jit(solution)/shard_map/project/pallas_call | solution.py:432
  69.9 12.0 %all_to_all.16 = bf16[16,2,5120]{2,1,0:T(2,128)(2,1)S(1)} all-to-all(bf16[16,2,5120]{2,1,0:T(2,128)(2,1)S(1)} %project.1), channel_id=1, replica_groups={{0,2,4,6,8,10,12,14,16,18,20,22,24,26,28,30},{1,3,5,7,9,11,13,15,17,19,..., dimensions={0} | all-to-all | bytes 655360 | tf_op jit(solution)/shard_map/send_rows/all_to_all | solution.py:444
  82.0 0.9 %reduce_sum.12 = bf16[2,5120]{1,0:T(2,128)(2,1)} reduce(bf16[16,2,5120]{2,1,0:T(2,128)(2,1)S(1)} %all_to_all.16, bf16[]{:T(256)} %constant.21.clone.1), dimensions={0}, to_apply=%region_0.1 | reduce | flops 153600 | bytes 348162 | tf_op jit(solution)/shard_map/send_rows/reduce_sum | solution.py:445
  (25 shorter events, 0.2 us)
Async XLA Ops:
  0.0 24.8 %copy-start.4 = (s32[2]{0:T(128)S(1)}, s32[2]{0:T(128)}, u32[]{:S(2)}) copy-start(s32[2]{0:T(128)} %counts_ref.3) | copy-start | bytes 28
  0.0 11.9 %collective-permute-start.1 = (bf16[256,640]{1,0:T(8,128)(2,1)}, bf16[256,640]{1,0:T(8,128)(2,1)S(1)}, u32[]{:S(2)}, u32[]{:S(2)}) collective-permute-start(bf16[256,640]{1,0:T(8,128)(2,1)} %rest_0_.1), channel_id=1, source_target_pairs={{0,1},{1,0},{2,3},{3,2},{4,5},{5,4},{6,7},{7,6},{8,9},{9,8},{10,11... | collective-permute-start | bytes 983048 | tf_op jit(solution)/shard_map/weights/ppermute | solution.py:304
  1.6 19.2 %all-to-all-start = ((bf16[16,2,8192]{2,1,0:T(2,128)(2,1)}), bf16[16,2,8192]{2,1,0:T(2,128)(2,1)S(1)}, u32[]{:S(2)}, u32[]{:S(2)}) async-start(bf16[16,2,8192]{2,1,0:T(2,128)(2,1)} %spread_queries.1), calls=%async_computation | async-start | bytes 1048576 | tf_op jit(solution)/shard_map/spread_queries/all_to_all | solution.py:329
  8.7 10.6 %collective-permute-start = (bf16[256,640]{1,0:T(8,128)(2,1)}, bf16[256,640]{1,0:T(8,128)(2,1)S(1)}, u32[]{:S(2)}, u32[]{:S(2)}) collective-permute-start(bf16[256,640]{1,0:T(8,128)(2,1)} %rest_0_.1), channel_id=1, source_target_pairs={{0,32},{1,225},{2,34},{3,227},{4,36},{5,229},{6,38},{7,231},{8,40}... | collective-permute-start | bytes 983048 | tf_op jit(solution)/shard_map/weights/ppermute | solution.py:312
  11.9 9.1 %collective-permute-start.2 = (bf16[256,640]{1,0:T(8,128)(2,1)S(1)}, bf16[256,640]{1,0:T(8,128)(2,1)S(1)}, u32[]{:S(2)}, u32[]{:S(2)}) collective-permute-start(bf16[256,640]{1,0:T(8,128)(2,1)S(1)} %collective-permute-done.1.rest_1_), channel_id=1, source_target_pairs={{0,32},{1,225},{2,34},{3,227},{4,36},{5,229},{6,38},{7,231},{8,40}... | collective-permute-start | bytes 983048 | tf_op jit(solution)/shard_map/weights/ppermute | solution.py:312
  14.1 10.7 %copy-start.3 = (s32[11]{0:T(128)S(1)}, s32[11]{0:T(128)}, u32[]{:S(2)}) copy-start(s32[11]{0:T(128)} %dynamic-slice_bitcast_fusion.info_ref) | copy-start | bytes 136
  21.1 3.7 %collective-permute-start.3 = (bf16[32,8192]{1,0:T(8,128)(2,1)S(1)}, bf16[32,8192]{1,0:T(8,128)(2,1)S(1)}, u32[]{:S(2)}, u32[]{:S(2)}) collective-permute-start(bf16[32,8192]{1,0:T(8,128)(2,1)S(1)} %reshape.3.q_own), channel_id=1, source_target_pairs={{0,1},{1,0},{2,3},{3,2},{4,5},{5,4},{6,7},{7,6},{8,9},{9,8},{10,11... | collective-permute-start | bytes 1572872 | tf_op jit(solution)/shard_map/spread_queries/ppermute | solution.py:304
  21.2 13.4 %collective-permute-start.5 = (bf16[512,640]{1,0:T(8,128)(2,1)S(1)}, bf16[512,640]{1,0:T(8,128)(2,1)S(1)}, u32[]{:S(2)}, u32[]{:S(2)}) collective-permute-start(bf16[512,640]{1,0:T(8,128)(2,1)S(1)} %constant_dynamic-update-slice_fusion.rest_2_), channel_id=1, source_target_pairs={{0,1},{1,0},{2,3},{3,2},{4,5},{5,4},{6,7},{7,6},{8,9},{9,8},{10,11... | collective-permute-start | bytes 1966088 | tf_op jit(solution)/shard_map/weights/ppermute | solution.py:304
  21.7 12.9 %collective-permute-start.4 = (bf16[512,640]{1,0:T(8,128)(2,1)S(1)}, bf16[512,640]{1,0:T(8,128)(2,1)S(1)}, u32[]{:S(2)}, u32[]{:S(2)}) collective-permute-start(bf16[512,640]{1,0:T(8,128)(2,1)S(1)} %constant_dynamic-update-slice_fusion.rest_2_), channel_id=1, source_target_pairs={{0,32},{1,225},{2,34},{3,227},{4,36},{5,229},{6,38},{7,231},{8,40}... | collective-permute-start | bytes 1966088 | tf_op jit(solution)/shard_map/weights/ppermute | solution.py:312
  24.8 0.9 %copy-start = (f32[8,16,384]{2,1,0:T(8,128)S(1)}, f32[8,16,384]{2,1,0:T(8,128)}, u32[]{:S(2)}) copy-start(f32[8,16,384]{2,1,0:T(8,128)} %suffix.1.suf_ref) | copy-start | bytes 589828
  34.5 9.2 %copy-start.1 = (f32[10,144,128]{2,1,0:T(8,128)S(1)}, f32[10,144,128]{2,1,0:T(8,128)}, u32[]{:S(2)}) copy-start(f32[10,144,128]{2,1,0:T(8,128)} %get-tuple-element.19.refs_0_) | copy-start | bytes 2211844
  34.5 33.5 %copy-start.2 = (bf16[256,640]{1,0:T(8,128)(2,1)S(1)}, bf16[256,640]{1,0:T(8,128)(2,1)}, u32[]{:S(2)}) copy-start(bf16[256,640]{1,0:T(8,128)(2,1)} %rest_0_.1) | copy-start | bytes 983044
  34.5 10.0 %collective-permute-start.9 = (bf16[512,640]{1,0:T(8,128)(2,1)S(1)}, bf16[512,640]{1,0:T(8,128)(2,1)S(1)}, u32[]{:S(2)}, u32[]{:S(2)}) collective-permute-start(bf16[512,640]{1,0:T(8,128)(2,1)S(1)} %collective-permute-done.4.rest_4_), channel_id=1, source_target_pairs={{0,1},{1,0},{2,3},{3,2},{4,5},{5,4},{6,7},{7,6},{8,9},{9,8},{10,11... | collective-permute-start | bytes 1966088 | tf_op jit(solution)/shard_map/weights/ppermute | solution.py:304
  34.6 10.7 %collective-permute-start.8 = (bf16[512,640]{1,0:T(8,128)(2,1)S(1)}, bf16[512,640]{1,0:T(8,128)(2,1)S(1)}, u32[]{:S(2)}, u32[]{:S(2)}) collective-permute-start(bf16[512,640]{1,0:T(8,128)(2,1)S(1)} %collective-permute-done.4.rest_4_), channel_id=1, source_target_pairs={{0,32},{1,225},{2,34},{3,227},{4,36},{5,229},{6,38},{7,231},{8,40}... | collective-permute-start | bytes 1966088 | tf_op jit(solution)/shard_map/weights/ppermute | solution.py:312
  36.7 7.0 %collective-permute-start.6 = (bf16[10,144,128]{2,1,0:T(8,128)(2,1)S(1)}, bf16[10,144,128]{2,1,0:T(8,128)(2,1)S(1)}, u32[]{:S(2)}, u32[]{:S(2)}) collective-permute-start(bf16[10,144,128]{2,1,0:T(8,128)(2,1)S(1)} %get-tuple-element.24), channel_id=1, source_target_pairs={{0,1},{1,0},{2,3},{3,2},{4,5},{5,4},{6,7},{7,6},{8,9},{9,8},{10,11... | collective-permute-start | bytes 1105928 | tf_op jit(solution)/shard_map/prefix/ppermute | solution.py:304
  42.0 1.7 %collective-permute-start.7 = (bf16[6,144,128]{2,1,0:T(8,128)(2,1)S(1)}, bf16[6,144,128]{2,1,0:T(8,128)(2,1)S(1)}, u32[]{:S(2)}, u32[]{:S(2)}) collective-permute-start(bf16[6,144,128]{2,1,0:T(8,128)(2,1)S(1)} %get-tuple-element.25), channel_id=1, source_target_pairs={{0,1},{1,0},{2,3},{3,2},{4,5},{5,4},{6,7},{7,6},{8,9},{9,8},{10,11... | collective-permute-start | bytes 663560 | tf_op jit(solution)/shard_map/prefix/ppermute | solution.py:304
  45.3 22.7 %collective-permute-start.11 = (bf16[512,640]{1,0:T(8,128)(2,1)S(1)}, bf16[512,640]{1,0:T(8,128)(2,1)S(1)}, u32[]{:S(2)}, u32[]{:S(2)}) collective-permute-start(bf16[512,640]{1,0:T(8,128)(2,1)S(1)} %collective-permute-done.8.rest_6_), channel_id=1, source_target_pairs={{0,32},{1,225},{2,34},{3,227},{4,36},{5,229},{6,38},{7,231},{8,40}... | collective-permute-start | bytes 1966088 | tf_op jit(solution)/shard_map/weights/ppermute | solution.py:312
  48.5 19.5 %collective-permute-start.10 = (bf16[512,640]{1,0:T(8,128)(2,1)S(1)}, bf16[512,640]{1,0:T(8,128)(2,1)S(1)}, u32[]{:S(2)}, u32[]{:S(2)}) collective-permute-start(bf16[512,640]{1,0:T(8,128)(2,1)S(1)} %collective-permute-done.8.rest_6_), channel_id=1, source_target_pairs={{0,1},{1,0},{2,3},{3,2},{4,5},{5,4},{6,7},{7,6},{8,9},{9,8},{10,11... | collective-permute-start | bytes 1966088 | tf_op jit(solution)/shard_map/weights/ppermute | solution.py:304
where the time goes:
time: 83.3 us; the launch traced here: 82.8 us
  blocking collectives  31.6 us (38%)
  Pallas kernels  23.6 us (28%)
  starting transfers between devices  20.8 us (25%)
  waiting for transfers between devices  3.35 us (4%)
  local copies, waits for them, and re-layouts  2.41 us (3%)
  other arithmetic  0.88 us (1%)
    all_to_all x1, blocking collectives, body(): lax.all_to_all(parts, 'ctx', 0, 0, tiled=True, axis_index_groups=same_core)  19.5 us
    pallas_call x2, Pallas kernels, body(): pl.pallas_call(prefix_kernel, out_shape=(jax.ShapeDtypeStruct((2 * heads,...  14.1 us
    ppermute x5, starting transfers between devices, along_z(): return lax.ppermute(x, ('group', 'ctx'), ring)  12.5 us
    all_to_all x1, blocking collectives, body(): lax.all_to_all(out, 'ctx', 0, 0, tiled=True, axis_index_groups=same_core)  12 us
    all_to_all x1, starting transfers between devices, body(): lax.all_to_all(spread, 'ctx', 0, 0, tiled=True, axis_index_groups=same_core)  7.03 us
    pallas_call x1, Pallas kernels, body(): pl.pallas_call(suffix_kernel, out_shape=jax.ShapeDtypeStruct((KVH, GQ * s...  5.18 us
    pallas_call x1, Pallas kernels, body(): pl.pallas_call(project_kernel, out_shape=jax.ShapeDtypeStruct((chips, sam...  1.89 us
  transfers between devices with their start and end apart: 13, of which 3 were waited for; matrix products, arithmetic and copies ran while one was open for 2% of the time, Pallas kernels for 26%

commit v1 on v0

--- a/solution.py
+++ b/solution.py
@@ -393,7 +393,7 @@
                 in_specs=[smem, smem, q_block, q_block, kv_block, kv_block, suf_block],
                 out_specs=(out_block, out_block),
                 scratch_shapes=[pltpu.VMEM((tiles, TILE, DH), f32)] * 3,
-                compiler_params=pltpu.CompilerParams(vmem_limit_bytes=52 * 2**20),
+                compiler_params=pltpu.CompilerParams(vmem_limit_bytes=48 * 2**20),
                 cost_estimate=pl.CostEstimate(
                     flops=2**31, bytes_accessed=2**23, transcendentals=2**22
                 ),
@@ -419,7 +419,7 @@
         )(*keeps, *recvs)
 
     with jax.named_scope("weights"):
-        parts, x3, e2 = lax.optimization_barrier((parts, x3, e2))
+        parts, e2 = lax.optimization_barrier((parts, e2))
         e3 = other_core(x3)
         x4 = along_z(x3)
         blocks = (out_weight, w_oth, x1, e1, x2, e2, x3, e3, x4)

time: 83.3 us -> 82.4 us (0.989); the launches traced: 82.8 us -> 80.9 us
  blocking collectives: 31.6 us -> 29.2 us
  starting transfers between devices: 20.8 us -> 21.7 us
    all_to_all x1, blocking collectives: 19.5 us -> 17.1 us  [body(): lax.all_to_all(parts, 'ctx', 0, 0, tiled=True, axis_index_groups=same_core)]
    ppermute x5, waiting for transfers between devices: 0.75 us -> 2.1 us  [along_z(): return lax.ppermute(x, ('group', 'ctx'), ring)]
    ppermute x7, waiting for transfers between devices: 1.12 us -> 0.02 us  [other_core(): return lax.ppermute(x, 'ctx', [(i, i ^ 1) for i in range(n_ctx)])]
    ppermute x5, starting transfers between devices: 12.5 us -> 13.6 us  [along_z(): return lax.ppermute(x, ('group', 'ctx'), ring)]
  transfers between devices with their start and end apart: 13 -> 13, of which waited for: 3 -> 2; matrix products, arithmetic and copies ran while one was open for 2% -> 2% of each run, Pallas kernels for 26% -> 26%
where the time goes in v1:
time: 82.4 us; the launch traced here: 80.9 us
  blocking collectives  29.2 us (35%)
  Pallas kernels  23 us (28%)
  starting transfers between devices  21.7 us (26%)
  waiting for transfers between devices  3.6 us (4%)
  local copies, waits for them, and re-layouts  2.41 us (3%)
  other arithmetic  0.88 us (1%)
    all_to_all x1, blocking collectives, body(): lax.all_to_all(parts, 'ctx', 0, 0, tiled=True, axis_index_groups=same_core)  17.1 us
    ppermute x5, starting transfers between devices, along_z(): return lax.ppermute(x, ('group', 'ctx'), ring)  13.6 us
    pallas_call x2, Pallas kernels, body(): pl.pallas_call(prefix_kernel, out_shape=(jax.ShapeDtypeStruct((2 * heads,...  13.4 us
    all_to_all x1, blocking collectives, body(): lax.all_to_all(out, 'ctx', 0, 0, tiled=True, axis_index_groups=same_core)  12 us
    all_to_all x1, starting transfers between devices, body(): lax.all_to_all(spread, 'ctx', 0, 0, tiled=True, axis_index_groups=same_core)  7.03 us
    pallas_call x1, Pallas kernels, body(): pl.pallas_call(suffix_kernel, out_shape=jax.ShapeDtypeStruct((KVH, GQ * s...  5.18 us
    ppermute x5, waiting for transfers between devices, along_z(): return lax.ppermute(x, ('group', 'ctx'), ring)  2.1 us
    pallas_call x1, Pallas kernels, body(): pl.pallas_call(project_kernel, out_shape=jax.ShapeDtypeStruct((chips, sam...  1.89 us
  transfers between devices with their start and end apart: 13, of which 2 were waited for; matrix products, arithmetic and copies ran while one was open for 2% of the time, Pallas kernels for 26%

profile of v1, /device:TPU:96, one launch (start us, length us, event | category | flops | bytes accessed | tf_op | source)
XLA Modules:
  0.0 80.9 jit_solution(5989367533201466485)
XLA Ops:
  0.0 1.6 %spread_queries.1 = bf16[16,2,8192]{2,1,0:T(2,128)(2,1)} custom-call(bf16[2,8192]{1,0:T(2,128)(2,1)} %q_hbm.1), custom_call_target="tpu_custom_call" | custom-call | flops 1 | bytes 524288 | tf_op jit(solution)/shard_map/spread_queries/pallas_call | solution.py:322
  1.6 7.0 %all-to-all-start = ((bf16[16,2,8192]{2,1,0:T(2,128)(2,1)}), bf16[16,2,8192]{2,1,0:T(2,128)(2,1)S(1)}, u32[]{:S(2)}, u32[]{:S(2)}) async-start(bf16[16,2,8192]{2,1,0:T(2,128)(2,1)} %spread_queries.1), calls=%async_computation | async-start | bytes 1048576 | tf_op jit(solution)/shard_map/spread_queries/all_to_all | solution.py:329
  8.7 3.2 %collective-permute-start = (bf16[256,640]{1,0:T(8,128)(2,1)}, bf16[256,640]{1,0:T(8,128)(2,1)S(1)}, u32[]{:S(2)}, u32[]{:S(2)}) collective-permute-start(bf16[256,640]{1,0:T(8,128)(2,1)} %rest_0_.1), channel_id=1, source_target_pairs={{0,32},{1,225},{2,34},{3,227},{4,36},{5,229},{6,38},{7,231},{8,40}... | collective-permute-start | bytes 983048 | tf_op jit(solution)/shard_map/weights/ppermute | solution.py:312
  11.9 1.0 %collective-permute-start.2 = (bf16[256,640]{1,0:T(8,128)(2,1)S(1)}, bf16[256,640]{1,0:T(8,128)(2,1)S(1)}, u32[]{:S(2)}, u32[]{:S(2)}) collective-permute-start(bf16[256,640]{1,0:T(8,128)(2,1)S(1)} %collective-permute-done.1.rest_1_), channel_id=1, source_target_pairs={{0,32},{1,225},{2,34},{3,227},{4,36},{5,229},{6,38},{7,231},{8,40}... | collective-permute-start | bytes 983048 | tf_op jit(solution)/shard_map/weights/ppermute | solution.py:312
  12.9 1.2 %dynamic-slice_bitcast_fusion.info_ref = s32[11]{0:T(128)} fusion(s32[256,11]{1,0:T(8,128)} %constant.22.clone, s32[]{:T(128)S(6)} %select_n.4), kind=kLoop, calls=%fused_computation.2 | loop fusion | bytes 92 | tf_op jit(solution)/shard_map/jit(dynamic_index_in_dim)/squeeze | solution.py:344
  14.1 5.2 %suffix.1.suf_ref = f32[8,16,384]{2,1,0:T(8,128)} custom-call(s32[2]{0:T(128)} %len_ref.1, s32[11]{0:T(128)} %dynamic-slice_bitcast_fusion.info_ref, bf16[2,8192]{1,0:T(2,128)(2,1)} %q_hbm.1, bf16[2,256,1024]{2,1,0:T(8,128)(2,1)} %sk_hbm.1, bf16[2,256,1024]{2,1,0:T(8,128)(2,1)} %sv_hbm.1, bf16[2,1024]{1,0:T(2,128)(2,1)} %nk_hbm.1, bf16[2,1024]{1,0:T(2,128)(2,1)} %nv_hbm.1), custom_call_target="tpu_custom_call" | custom-call | flops 1 | bytes 1 | tf_op jit(solution)/shard_map/suffix/pallas_call | solution.py:350
  19.3 1.5 %all-to-all-done = bf16[16,2,8192]{2,1,0:T(2,128)(2,1)S(1)} async-done(((bf16[16,2,8192]{2,1,0:T(2,128)(2,1)}), bf16[16,2,8192]{2,1,0:T(2,128)(2,1)S(1)}, u32[]{:S(2)}, u32[]{:S(2)}) %all-to-all-start) | async-done | bytes 524320 | tf_op jit(solution)/shard_map/spread_queries/all_to_all | solution.py:329
  20.8 0.2 reshape.3.q_own
  21.1 0.1 collective-permute-start.3
  21.2 3.2 %collective-permute-start.4 = (bf16[512,640]{1,0:T(8,128)(2,1)S(1)}, bf16[512,640]{1,0:T(8,128)(2,1)S(1)}, u32[]{:S(2)}, u32[]{:S(2)}) collective-permute-start(bf16[512,640]{1,0:T(8,128)(2,1)S(1)} %constant_dynamic-update-slice_fusion.rest_2_), channel_id=1, source_target_pairs={{0,32},{1,225},{2,34},{3,227},{4,36},{5,229},{6,38},{7,231},{8,40}... | collective-permute-start | bytes 1966088 | tf_op jit(solution)/shard_map/weights/ppermute | solution.py:312
  24.4 0.9 %copy-done.1 = f32[8,16,384]{2,1,0:T(8,128)S(1)} copy-done((f32[8,16,384]{2,1,0:T(8,128)S(1)}, f32[8,16,384]{2,1,0:T(8,128)}, u32[]{:S(2)}) %copy-start.1) | copy-done | bytes 196632
  25.3 8.0 %prefix.2 = (f32[10,144,128]{2,1,0:T(8,128)S(1)}, bf16[10,144,128]{2,1,0:T(8,128)(2,1)S(1)}) custom-call(s32[11]{0:T(128)S(1)} %copy-done.3, s32[2]{0:T(128)S(1)} %copy-done.4, bf16[32,8192]{1,0:T(8,128)(2,1)S(1)} %reshape.3.q_own, bf16[32,8192]{1,0:T(8,128)(2,1)S(1)} %collective-permute-done.3.q_oth, bf16[2,1024,1024]{2,1,0:T(8,128)(2,1)} %k_ref.3, ...), custom_call_target="tpu_custom_call" | custom-call | flops 2147483648 | bytes 8388608 | tf_op jit(solution)/shard_map/prefix/pallas_call | solution.py:386
  33.4 2.8 %collective-permute-start.9 = (bf16[512,640]{1,0:T(8,128)(2,1)S(1)}, bf16[512,640]{1,0:T(8,128)(2,1)S(1)}, u32[]{:S(2)}, u32[]{:S(2)}) collective-permute-start(bf16[512,640]{1,0:T(8,128)(2,1)S(1)} %collective-permute-done.4.rest_4_), channel_id=1, source_target_pairs={{0,32},{1,225},{2,34},{3,227},{4,36},{5,229},{6,38},{7,231},{8,40}... | collective-permute-start | bytes 1966088 | tf_op jit(solution)/shard_map/weights/ppermute | solution.py:312
  36.2 0.5 collective-permute-start.6
  36.7 5.4 %prefix.3 = (f32[6,144,128]{2,1,0:T(8,128)S(1)}, bf16[6,144,128]{2,1,0:T(8,128)(2,1)S(1)}) custom-call(s32[11]{0:T(128)S(1)} %copy-done.3, s32[2]{0:T(128)S(1)} %copy-done.4, bf16[32,8192]{1,0:T(8,128)(2,1)S(1)} %reshape.3.q_own, bf16[32,8192]{1,0:T(8,128)(2,1)S(1)} %collective-permute-done.3.q_oth, bf16[2,1024,1024]{2,1,0:T(8,128)(2,1)S(1)} %copy-done, ...), custom_call_target="tpu_custom_call" | custom-call | flops 2147483648 | bytes 8388608 | tf_op jit(solution)/shard_map/prefix/pallas_call | solution.py:386
  42.1 0.1 collective-permute-start.7
  42.2 2.1 %collective-permute-done.9.rest_6_ = bf16[512,640]{1,0:T(8,128)(2,1)S(1)} collective-permute-done((bf16[512,640]{1,0:T(8,128)(2,1)S(1)}, bf16[512,640]{1,0:T(8,128)(2,1)S(1)}, u32[]{:S(2)}, u32[]{:S(2)}) %collective-permute-start.9) | collective-permute-done | bytes 655392 | tf_op jit(solution)/shard_map/weights/ppermute | solution.py:312
  44.3 0.3 collective-permute-start.10
  44.6 3.4 %collective-permute-start.11 = (bf16[512,640]{1,0:T(8,128)(2,1)S(1)}, bf16[512,640]{1,0:T(8,128)(2,1)S(1)}, u32[]{:S(2)}, u32[]{:S(2)}) collective-permute-start(bf16[512,640]{1,0:T(8,128)(2,1)S(1)} %collective-permute-done.9.rest_6_), channel_id=1, source_target_pairs={{0,32},{1,225},{2,34},{3,227},{4,36},{5,229},{6,38},{7,231},{8,40}... | collective-permute-start | bytes 1966088 | tf_op jit(solution)/shard_map/weights/ppermute | solution.py:312
  48.0 0.9 %join_cores.1 = bf16[16,144,128]{2,1,0:T(8,128)(2,1)S(1)} custom-call(f32[10,144,128]{2,1,0:T(8,128)S(1)} %get-tuple-element.18.refs_0_, f32[6,144,128]{2,1,0:T(8,128)S(1)} %get-tuple-element.22.refs_1_, bf16[10,144,128]{2,1,0:T(8,128)(2,1)S(1)} %collective-permute-done.6.refs_2_, bf16[6,144,128]{2,1,0:T(8,128)(2,1)S(1)} %collective-permute-done.7.refs_3_), custom_call_target="tpu_custom_call" | custom-call | tf_op jit(solution)/shard_map/join_cores/pallas_call | solution.py:413
  48.9 17.1 %all_to_all.15.parts_ref = bf16[16,144,128]{2,1,0:T(8,128)(2,1)S(1)} all-to-all(bf16[16,144,128]{2,1,0:T(8,128)(2,1)S(1)} %join_cores.1), channel_id=1, replica_groups={{0,2,4,6,8,10,12,14,16,18,20,22,24,26,28,30},{1,3,5,7,9,11,13,15,17,19,..., dimensions={0} | all-to-all | bytes 1179648 | tf_op jit(solution)/shard_map/send_parts/all_to_all | solution.py:428
  66.0 1.9 %project.1 = bf16[16,2,5120]{2,1,0:T(2,128)(2,1)S(1)} custom-call(s32[11]{0:T(128)S(1)} %copy-done.3, bf16[16,144,128]{2,1,0:T(8,128)(2,1)S(1)} %all_to_all.15.parts_ref, bf16[256,640]{1,0:T(8,128)(2,1)S(1)} %copy-done.2, bf16[256,640]{1,0:T(8,128)(2,1)S(1)} %collective-permute-done.1.rest_1_, ...), custom_call_target="tpu_custom_call" | custom-call | flops 268435456 | bytes 8388608 | tf_op jit(solution)/shard_map/project/pallas_call | solution.py:432
  67.9 12.0 %all_to_all.16 = bf16[16,2,5120]{2,1,0:T(2,128)(2,1)S(1)} all-to-all(bf16[16,2,5120]{2,1,0:T(2,128)(2,1)S(1)} %project.1), channel_id=1, replica_groups={{0,2,4,6,8,10,12,14,16,18,20,22,24,26,28,30},{1,3,5,7,9,11,13,15,17,19,..., dimensions={0} | all-to-all | bytes 655360 | tf_op jit(solution)/shard_map/send_rows/all_to_all | solution.py:444
  80.0 0.9 %reduce_sum.12 = bf16[2,5120]{1,0:T(2,128)(2,1)} reduce(bf16[16,2,5120]{2,1,0:T(2,128)(2,1)S(1)} %all_to_all.16, bf16[]{:T(256)} %constant.21.clone.1), dimensions={0}, to_apply=%region_0.1 | reduce | flops 153600 | bytes 348162 | tf_op jit(solution)/shard_map/send_rows/reduce_sum | solution.py:445
  (25 shorter events, 0.1 us)
Async XLA Ops:
  0.0 24.4 %copy-start.4 = (s32[2]{0:T(128)S(1)}, s32[2]{0:T(128)}, u32[]{:S(2)}) copy-start(s32[2]{0:T(128)} %counts_ref.3) | copy-start | bytes 28
  0.0 11.9 %collective-permute-start.1 = (bf16[256,640]{1,0:T(8,128)(2,1)}, bf16[256,640]{1,0:T(8,128)(2,1)S(1)}, u32[]{:S(2)}, u32[]{:S(2)}) collective-permute-start(bf16[256,640]{1,0:T(8,128)(2,1)} %rest_0_.1), channel_id=1, source_target_pairs={{0,1},{1,0},{2,3},{3,2},{4,5},{5,4},{6,7},{7,6},{8,9},{9,8},{10,11... | collective-permute-start | bytes 983048 | tf_op jit(solution)/shard_map/weights/ppermute | solution.py:304
  1.6 19.2 %all-to-all-start = ((bf16[16,2,8192]{2,1,0:T(2,128)(2,1)}), bf16[16,2,8192]{2,1,0:T(2,128)(2,1)S(1)}, u32[]{:S(2)}, u32[]{:S(2)}) async-start(bf16[16,2,8192]{2,1,0:T(2,128)(2,1)} %spread_queries.1), calls=%async_computation | async-start | bytes 1048576 | tf_op jit(solution)/shard_map/spread_queries/all_to_all | solution.py:329
  8.7 10.6 %collective-permute-start = (bf16[256,640]{1,0:T(8,128)(2,1)}, bf16[256,640]{1,0:T(8,128)(2,1)S(1)}, u32[]{:S(2)}, u32[]{:S(2)}) collective-permute-start(bf16[256,640]{1,0:T(8,128)(2,1)} %rest_0_.1), channel_id=1, source_target_pairs={{0,32},{1,225},{2,34},{3,227},{4,36},{5,229},{6,38},{7,231},{8,40}... | collective-permute-start | bytes 983048 | tf_op jit(solution)/shard_map/weights/ppermute | solution.py:312
  11.9 9.1 %collective-permute-start.2 = (bf16[256,640]{1,0:T(8,128)(2,1)S(1)}, bf16[256,640]{1,0:T(8,128)(2,1)S(1)}, u32[]{:S(2)}, u32[]{:S(2)}) collective-permute-start(bf16[256,640]{1,0:T(8,128)(2,1)S(1)} %collective-permute-done.1.rest_1_), channel_id=1, source_target_pairs={{0,32},{1,225},{2,34},{3,227},{4,36},{5,229},{6,38},{7,231},{8,40}... | collective-permute-start | bytes 983048 | tf_op jit(solution)/shard_map/weights/ppermute | solution.py:312
  14.1 10.3 %copy-start.3 = (s32[11]{0:T(128)S(1)}, s32[11]{0:T(128)}, u32[]{:S(2)}) copy-start(s32[11]{0:T(128)} %dynamic-slice_bitcast_fusion.info_ref) | copy-start | bytes 136
  21.1 15.6 %copy-start = (bf16[2,1024,1024]{2,1,0:T(8,128)(2,1)S(1)}, bf16[2,1024,1024]{2,1,0:T(8,128)(2,1)}, u32[]{:S(2)}) copy-start(bf16[2,1024,1024]{2,1,0:T(8,128)(2,1)} %k_ref.3) | copy-start | bytes 12582916
  21.1 3.3 %collective-permute-start.3 = (bf16[32,8192]{1,0:T(8,128)(2,1)S(1)}, bf16[32,8192]{1,0:T(8,128)(2,1)S(1)}, u32[]{:S(2)}, u32[]{:S(2)}) collective-permute-start(bf16[32,8192]{1,0:T(8,128)(2,1)S(1)} %reshape.3.q_own), channel_id=1, source_target_pairs={{0,1},{1,0},{2,3},{3,2},{4,5},{5,4},{6,7},{7,6},{8,9},{9,8},{10,11... | collective-permute-start | bytes 1572872 | tf_op jit(solution)/shard_map/spread_queries/ppermute | solution.py:304
  21.2 12.2 %collective-permute-start.4 = (bf16[512,640]{1,0:T(8,128)(2,1)S(1)}, bf16[512,640]{1,0:T(8,128)(2,1)S(1)}, u32[]{:S(2)}, u32[]{:S(2)}) collective-permute-start(bf16[512,640]{1,0:T(8,128)(2,1)S(1)} %constant_dynamic-update-slice_fusion.rest_2_), channel_id=1, source_target_pairs={{0,32},{1,225},{2,34},{3,227},{4,36},{5,229},{6,38},{7,231},{8,40}... | collective-permute-start | bytes 1966088 | tf_op jit(solution)/shard_map/weights/ppermute | solution.py:312
  24.4 9.0 %collective-permute-start.5 = (bf16[512,640]{1,0:T(8,128)(2,1)S(1)}, bf16[512,640]{1,0:T(8,128)(2,1)S(1)}, u32[]{:S(2)}, u32[]{:S(2)}) collective-permute-start(bf16[512,640]{1,0:T(8,128)(2,1)S(1)} %constant_dynamic-update-slice_fusion.rest_2_), channel_id=1, source_target_pairs={{0,1},{1,0},{2,3},{3,2},{4,5},{5,4},{6,7},{7,6},{8,9},{9,8},{10,11... | collective-permute-start | bytes 1966088 | tf_op jit(solution)/shard_map/weights/ppermute | solution.py:304
  24.4 0.9 %copy-start.1 = (f32[8,16,384]{2,1,0:T(8,128)S(1)}, f32[8,16,384]{2,1,0:T(8,128)}, u32[]{:S(2)}) copy-start(f32[8,16,384]{2,1,0:T(8,128)} %suffix.1.suf_ref) | copy-start | bytes 589828
  33.4 32.7 %copy-start.2 = (bf16[256,640]{1,0:T(8,128)(2,1)S(1)}, bf16[256,640]{1,0:T(8,128)(2,1)}, u32[]{:S(2)}) copy-start(bf16[256,640]{1,0:T(8,128)(2,1)} %rest_0_.1) | copy-start | bytes 983044
  33.4 10.9 %collective-permute-start.9 = (bf16[512,640]{1,0:T(8,128)(2,1)S(1)}, bf16[512,640]{1,0:T(8,128)(2,1)S(1)}, u32[]{:S(2)}, u32[]{:S(2)}) collective-permute-start(bf16[512,640]{1,0:T(8,128)(2,1)S(1)} %collective-permute-done.4.rest_4_), channel_id=1, source_target_pairs={{0,32},{1,225},{2,34},{3,227},{4,36},{5,229},{6,38},{7,231},{8,40}... | collective-permute-start | bytes 1966088 | tf_op jit(solution)/shard_map/weights/ppermute | solution.py:312
  36.2 12.7 %collective-permute-start.8 = (bf16[512,640]{1,0:T(8,128)(2,1)S(1)}, bf16[512,640]{1,0:T(8,128)(2,1)S(1)}, u32[]{:S(2)}, u32[]{:S(2)}) collective-permute-start(bf16[512,640]{1,0:T(8,128)(2,1)S(1)} %collective-permute-done.4.rest_4_), channel_id=1, source_target_pairs={{0,1},{1,0},{2,3},{3,2},{4,5},{5,4},{6,7},{7,6},{8,9},{9,8},{10,11... | collective-permute-start | bytes 1966088 | tf_op jit(solution)/shard_map/weights/ppermute | solution.py:304
  36.2 11.8 %collective-permute-start.6 = (bf16[10,144,128]{2,1,0:T(8,128)(2,1)S(1)}, bf16[10,144,128]{2,1,0:T(8,128)(2,1)S(1)}, u32[]{:S(2)}, u32[]{:S(2)}) collective-permute-start(bf16[10,144,128]{2,1,0:T(8,128)(2,1)S(1)} %get-tuple-element.23), channel_id=1, source_target_pairs={{0,1},{1,0},{2,3},{3,2},{4,5},{5,4},{6,7},{7,6},{8,9},{9,8},{10,11... | collective-permute-start | bytes 1105928 | tf_op jit(solution)/shard_map/prefix/ppermute | solution.py:304
  42.1 5.9 %collective-permute-start.7 = (bf16[6,144,128]{2,1,0:T(8,128)(2,1)S(1)}, bf16[6,144,128]{2,1,0:T(8,128)(2,1)S(1)}, u32[]{:S(2)}, u32[]{:S(2)}) collective-permute-start(bf16[6,144,128]{2,1,0:T(8,128)(2,1)S(1)} %get-tuple-element.24), channel_id=1, source_target_pairs={{0,1},{1,0},{2,3},{3,2},{4,5},{5,4},{6,7},{7,6},{8,9},{9,8},{10,11... | collective-permute-start | bytes 663560 | tf_op jit(solution)/shard_map/prefix/ppermute | solution.py:304
  44.3 21.7 %collective-permute-start.10 = (bf16[512,640]{1,0:T(8,128)(2,1)S(1)}, bf16[512,640]{1,0:T(8,128)(2,1)S(1)}, u32[]{:S(2)}, u32[]{:S(2)}) collective-permute-start(bf16[512,640]{1,0:T(8,128)(2,1)S(1)} %collective-permute-done.9.rest_6_), channel_id=1, source_target_pairs={{0,1},{1,0},{2,3},{3,2},{4,5},{5,4},{6,7},{7,6},{8,9},{9,8},{10,11... | collective-permute-start | bytes 1966088 | tf_op jit(solution)/shard_map/weights/ppermute | solution.py:304
  44.6 21.4 %collective-permute-start.11 = (bf16[512,640]{1,0:T(8,128)(2,1)S(1)}, bf16[512,640]{1,0:T(8,128)(2,1)S(1)}, u32[]{:S(2)}, u32[]{:S(2)}) collective-permute-start(bf16[512,640]{1,0:T(8,128)(2,1)S(1)} %collective-permute-done.9.rest_6_), channel_id=1, source_target_pairs={{0,32},{1,225},{2,34},{3,227},{4,36},{5,229},{6,38},{7,231},{8,40}... | collective-permute-start | bytes 1966088 | tf_op jit(solution)/shard_map/weights/ppermute | solution.py:312
